TPU v7x, 32 devices: a whole 2x2x4 slice. The times are simulated.
32 devices in a mesh: gx: 8 (over z, y), gy: 4 (over x, core).
Axes of the slice: x: 2, y: 2, z: 4, core: 2. Of those that a mesh axis runs over, the one named last changes fastest.
Arguments:
- spins: bfloat16 [16, 32, 256, 256], P(None, 'gx', 'gy'), may hold values from -1 to 1
- couplings: int32 [6, 32, 256, 256], P(None, 'gx', 'gy'), may hold values from -1 to 1, as said below
- betas: float32 [16], replicated, may hold values from 0.25 to 1.5
- metro_uniform: bfloat16 [2, 16, 32, 256, 256], P(None, None, 'gx', 'gy'), may hold values from 0 to 1
- swap_uniform: float32 [8], replicated, may hold values from 0.8 to 1
Outputs:
- spins_out: bfloat16 [16, 32, 256, 256], P(None, 'gx', 'gy')
- energies: float32 [16], replicated
Inputs may be any that keep to these rules, and one draw needn't show every extreme that they name: Every entry is -1 or 1; couplings[3 + d] at a cell equals couplings[d] at the cell one step lower along lattice dimension d, with periodic wrap.
All inputs are finite; a program needn't handle non-finite values.
Results may differ from a plain program's by a relative error of at most 0.0085.
Values may be sent and summed in bfloat16 or wider, within the bound.
A program may use at most 128 MiB of HBM per device.

v0:
```python
import jax
import jax.numpy as jnp
from jax import lax
from jax.sharding import PartitionSpec as P

SWEEPS = 2


soft_width = 0.1
swap_width = 0.25
swap_gain = 64.0


def with_halo(cells, sides, width):
    for axis, dim in sides:
        count = lax.axis_size(axis)
        head = lax.slice_in_dim(cells, 0, width, axis=dim)
        tail = lax.slice_in_dim(cells, cells.shape[dim] - width, cells.shape[dim], axis=dim)
        cells = jnp.concatenate(
            [
                lax.ppermute(tail, axis, [(i, (i + 1) % count) for i in range(count)]),
                cells,
                lax.ppermute(head, axis, [((i + 1) % count, i) for i in range(count)]),
            ],
            axis=dim,
        )
    return cells


def full_neighbours(state):
    padded = with_halo(state, (("gx", 1), ("gy", 2)), 1)
    return (padded[:, 2:, 1:-1], padded[:, :-2, 1:-1], padded[:, 1:-1, 2:], padded[:, 1:-1, :-2])


def neighbour_field(bonds, near, current):
    up_x, down_x, up_y, down_y = near
    field = bonds[0] * up_x.astype(jnp.float32) + bonds[3] * down_x.astype(jnp.float32)
    field = field + bonds[1] * up_y.astype(jnp.float32) + bonds[4] * down_y.astype(jnp.float32)
    field = field + bonds[2] * jnp.roll(current, -1, 3) + bonds[5] * jnp.roll(current, 1, 3)
    return field


def body(spins, couplings, betas, metro_uniform, swap_uniform):
    bonds = couplings.astype(jnp.float32)[:, None]
    replicas, cells_x, cells_y, cells_z = spins.shape
    shape = (cells_x, cells_y, cells_z)
    xstart = lax.axis_index("gx") * cells_x
    ystart = lax.axis_index("gy") * cells_y
    xcoord = xstart + lax.broadcasted_iota(jnp.int32, shape, 0)
    ycoord = ystart + lax.broadcasted_iota(jnp.int32, shape, 1)
    parity = (xcoord + ycoord + lax.broadcasted_iota(jnp.int32, shape, 2)) % 2
    inverse = betas[:, None, None, None]
    state = spins
    field = None
    for sweep in range(SWEEPS):
        uniform = metro_uniform[sweep].astype(jnp.float32)
        for colour in (0, 1):
            near = full_neighbours(state)
            current = state.astype(jnp.float32)
            field = neighbour_field(bonds, near, current)
            accept = jnp.exp(-inverse * jnp.maximum(2.0 * current * field, 0.0))
            weight = jax.nn.sigmoid((accept - uniform) / soft_width)
            flipped = current * (1.0 - 2.0 * weight)
            state = jnp.where(parity == colour, flipped, current).astype(jnp.bfloat16)
    current = state.astype(jnp.float32)
    partial_sum = jnp.sum(jnp.where(parity == 1, current * field, 0.0), axis=(1, 2, 3))
    total = lax.psum(partial_sum, ("gx", "gy"))
    cell_count = cells_x * lax.axis_size("gx") * cells_y * lax.axis_size("gy") * cells_z
    energies = -total / jnp.float32(cell_count)
    delta = swap_gain * (betas[0::2] - betas[1::2]) * (energies[0::2] - energies[1::2])
    mix = jax.nn.sigmoid((jnp.minimum(delta, 0.0) - jnp.log(swap_uniform)) / swap_width)
    paired = current.reshape(replicas // 2, 2, cells_x, cells_y, cells_z)
    weight = mix[:, None, None, None]
    upper = paired[:, 0]
    lower = paired[:, 1]
    new_upper = (1.0 - weight) * upper + weight * lower
    new_lower = (1.0 - weight) * lower + weight * upper
    mixed = jnp.stack([new_upper, new_lower], axis=1).astype(jnp.bfloat16)
    return (mixed.reshape(replicas, cells_x, cells_y, cells_z), energies)


def solution(mesh):
    in_specs = (
        P(None, "gx", "gy", None),
        P(None, "gx", "gy", None),
        P(),
        P(None, None, "gx", "gy", None),
        P(),
    )
    out_specs = (P(None, "gx", "gy", None), P())
    return jax.shard_map(body, mesh=mesh, in_specs=in_specs, out_specs=out_specs, check_vma=False)
```

profile of v0, /device:TPU:0, one launch (start us, length us, event | category | flops | bytes accessed | tf_op | source)
XLA Modules:
  0.0 215.8 jit_solution(15043850329621948405)
XLA Ops:
  0.6 2.4 %fusion.67 = (bf16[16,1,64,256]{3,2,1,0:T(8,128)(2,1)}, bf16[16,1,64,256]{3,2,1,0:T(8,128)(2,1)}) fusion(bf16[16,4,64,256]{3,2,1,0:T(8,128)(2,1)} %param.5), kind=kLoop, calls=%fused_computation.140 | loop fusion | bytes 2097152 | tf_op jit(solution)/shard_map/slice | solution.py:17
  3.1 3.0 %collective-permute-start.1 = (bf16[16,1,64,256]{3,2,1,0:T(8,128)(2,1)}, bf16[16,1,64,256]{3,2,1,0:T(8,128)(2,1)}, u32[]{:S(2)}, u32[]{:S(2)}) collective-permute-start(bf16[16,1,64,256]{3,2,1,0:T(8,128)(2,1)} %get-tuple-element.35), channel_id=1, source_target_pairs={{0,4},{4,8},{8,12},{12,16},{16,20},{20,24},{24,28},{28,0},{1,5},{5... | collective-permute-start | bytes 1572872 | tf_op jit(solution)/shard_map/ppermute | solution.py:21
  6.0 3.0 %collective-permute-start = (bf16[16,1,64,256]{3,2,1,0:T(8,128)(2,1)}, bf16[16,1,64,256]{3,2,1,0:T(8,128)(2,1)}, u32[]{:S(2)}, u32[]{:S(2)}) collective-permute-start(bf16[16,1,64,256]{3,2,1,0:T(8,128)(2,1)} %get-tuple-element.34), channel_id=1, source_target_pairs={{4,0},{8,4},{12,8},{16,12},{20,16},{24,20},{28,24},{0,28},{5,1},{9... | collective-permute-start | bytes 1572872 | tf_op jit(solution)/shard_map/ppermute | solution.py:23
  9.1 4.3 %fusion.68 = (f32[16,4,64,255]{3,2,1,0:T(8,128)}, f32[16,4,64,255]{3,2,1,0:T(8,128)}) fusion(bf16[16,4,64,256]{3,2,1,0:T(8,128)(2,1)S(1)} %copy-done), kind=kLoop, calls=%fused_computation.141 | loop fusion | bytes 16711680 | tf_op jit(solution)/shard_map/jit(_roll_static)/slice | solution.py:39
  16.3 12.5 %collective-permute-done.1 = bf16[16,1,64,256]{3,2,1,0:T(8,128)(2,1)} collective-permute-done((bf16[16,1,64,256]{3,2,1,0:T(8,128)(2,1)}, bf16[16,1,64,256]{3,2,1,0:T(8,128)(2,1)}, u32[]{:S(2)}, u32[]{:S(2)}) %collective-permute-start.1) | collective-permute-done | bytes 524320 | tf_op jit(solution)/shard_map/ppermute | solution.py:21
  33.1 1.4 collective-permute-done.2
  34.5 2.9 %collective-permute-done.3 = bf16[16,6,1,256]{3,2,1,0:T(2,128)(2,1)S(1)} collective-permute-done((bf16[16,6,1,256]{3,2,1,0:T(2,128)(2,1)S(1)}, bf16[16,6,1,256]{3,2,1,0:T(2,128)(2,1)S(1)}, u32[]{:S(2)}, u32[]{:S(2)}) %collective-permute-start.3) | collective-permute-done | bytes 49184 | tf_op jit(solution)/shard_map/ppermute | solution.py:21
  37.4 9.7 %fusion.49 = bf16[16,4,64,256]{3,2,1,0:T(8,128)(2,1)S(1)} fusion(f32[16,4,64,255]{3,2,1,0:T(8,128)S(1)} %copy-done.4, f32[16,4,64,1]{3,2,1,0:T(8,128)S(1)} %get-tuple-element.39, f32[16,4,64,1]{3,2,1,0:T(8,128)S(1)} %get-tuple-element.38, f32[16,4,64,255]{3,2,1,0:T(8,128)S(1)} %copy-done.3, ...), kind=kLoop, calls=%fused_computation.66 | loop fusion | flops 47185920 | bytes 20611136 | tf_op jit(solution)/shard_map/convert_element_type | solution.py:64
  47.3 4.6 %collective-permute-start.4 = (bf16[16,1,64,256]{3,2,1,0:T(8,128)(2,1)S(1)}, bf16[16,1,64,256]{3,2,1,0:T(8,128)(2,1)S(1)}, u32[]{:S(2)}, u32[]{:S(2)}) collective-permute-start(bf16[16,1,64,256]{3,2,1,0:T(8,128)(2,1)S(1)} %get-tuple-element.29), channel_id=1, source_target_pairs={{4,0},{8,4},{12,8},{16,12},{20,16},{24,20},{28,24},{0,28},{5,1},{9... | collective-permute-start | bytes 1572872 | tf_op jit(solution)/shard_map/ppermute | solution.py:23
  53.2 19.3 %collective-permute-done.4 = bf16[16,1,64,256]{3,2,1,0:T(8,128)(2,1)S(1)} collective-permute-done((bf16[16,1,64,256]{3,2,1,0:T(8,128)(2,1)S(1)}, bf16[16,1,64,256]{3,2,1,0:T(8,128)(2,1)S(1)}, u32[]{:S(2)}, u32[]{:S(2)}) %collective-permute-start.4) | collective-permute-done | bytes 524320 | tf_op jit(solution)/shard_map/ppermute | solution.py:23
  74.9 2.9 %collective-permute-done.7 = bf16[16,6,1,256]{3,2,1,0:T(2,128)(2,1)S(1)} collective-permute-done((bf16[16,6,1,256]{3,2,1,0:T(2,128)(2,1)S(1)}, bf16[16,6,1,256]{3,2,1,0:T(2,128)(2,1)S(1)}, u32[]{:S(2)}, u32[]{:S(2)}) %collective-permute-start.7) | collective-permute-done | bytes 49184 | tf_op jit(solution)/shard_map/ppermute | solution.py:21
  77.8 9.2 %fusion.50 = bf16[16,4,64,256]{3,2,1,0:T(8,128)(2,1)S(1)} fusion(f32[16,4,64,255]{3,2,1,0:T(8,128)S(1)} %get-tuple-element.31, f32[16,4,64,1]{3,2,1,0:T(8,128)S(1)} %get-tuple-element.33, f32[16,4,64,1]{3,2,1,0:T(8,128)S(1)} %get-tuple-element.32, f32[16,4,64,255]{3,2,1,0:T(8,128)S(1)} %get-tuple-element.30, ...), kind=kLoop, calls=%fused_computation.67 | loop fusion | flops 55574528 | bytes 17465408 | tf_op jit(solution)/shard_map/convert_element_type | solution.py:64
  87.1 4.6 %collective-permute-start.8 = (bf16[16,1,64,256]{3,2,1,0:T(8,128)(2,1)S(1)}, bf16[16,1,64,256]{3,2,1,0:T(8,128)(2,1)S(1)}, u32[]{:S(2)}, u32[]{:S(2)}) collective-permute-start(bf16[16,1,64,256]{3,2,1,0:T(8,128)(2,1)S(1)} %get-tuple-element.23), channel_id=1, source_target_pairs={{4,0},{8,4},{12,8},{16,12},{20,16},{24,20},{28,24},{0,28},{5,1},{9... | collective-permute-start | bytes 1572872 | tf_op jit(solution)/shard_map/ppermute | solution.py:23
  93.1 19.8 %collective-permute-done.8 = bf16[16,1,64,256]{3,2,1,0:T(8,128)(2,1)S(1)} collective-permute-done((bf16[16,1,64,256]{3,2,1,0:T(8,128)(2,1)S(1)}, bf16[16,1,64,256]{3,2,1,0:T(8,128)(2,1)S(1)}, u32[]{:S(2)}, u32[]{:S(2)}) %collective-permute-start.8) | collective-permute-done | bytes 524320 | tf_op jit(solution)/shard_map/ppermute | solution.py:23
  115.5 3.1 %collective-permute-done.11 = bf16[16,6,1,256]{3,2,1,0:T(2,128)(2,1)S(1)} collective-permute-done((bf16[16,6,1,256]{3,2,1,0:T(2,128)(2,1)S(1)}, bf16[16,6,1,256]{3,2,1,0:T(2,128)(2,1)S(1)}, u32[]{:S(2)}, u32[]{:S(2)}) %collective-permute-start.11) | collective-permute-done | bytes 49184 | tf_op jit(solution)/shard_map/ppermute | solution.py:21
  118.6 9.2 %fusion.51 = bf16[16,4,64,256]{3,2,1,0:T(8,128)(2,1)S(1)} fusion(f32[16,4,64,255]{3,2,1,0:T(8,128)S(1)} %get-tuple-element.25, f32[16,4,64,1]{3,2,1,0:T(8,128)S(1)} %get-tuple-element.27, f32[16,4,64,1]{3,2,1,0:T(8,128)S(1)} %get-tuple-element.26, f32[16,4,64,255]{3,2,1,0:T(8,128)S(1)} %get-tuple-element.24, ...), kind=kLoop, calls=%fused_computation.68 | loop fusion | flops 55574528 | bytes 17465408 | tf_op jit(solution)/shard_map/convert_element_type | solution.py:64
  128.7 3.0 %collective-permute-start.12 = (bf16[16,1,64,256]{3,2,1,0:T(8,128)(2,1)}, bf16[16,1,64,256]{3,2,1,0:T(8,128)(2,1)}, u32[]{:S(2)}, u32[]{:S(2)}) collective-permute-start(bf16[16,1,64,256]{3,2,1,0:T(8,128)(2,1)} %get-tuple-element.17), channel_id=1, source_target_pairs={{4,0},{8,4},{12,8},{16,12},{20,16},{24,20},{28,24},{0,28},{5,1},{9... | collective-permute-start | bytes 1572872 | tf_op jit(solution)/shard_map/ppermute | solution.py:23
  133.3 21.6 %collective-permute-done.12 = bf16[16,1,64,256]{3,2,1,0:T(8,128)(2,1)} collective-permute-done((bf16[16,1,64,256]{3,2,1,0:T(8,128)(2,1)}, bf16[16,1,64,256]{3,2,1,0:T(8,128)(2,1)}, u32[]{:S(2)}, u32[]{:S(2)}) %collective-permute-start.12) | collective-permute-done | bytes 524320 | tf_op jit(solution)/shard_map/ppermute | solution.py:23
  157.2 1.5 collective-permute-done.14
  158.7 2.2 %collective-permute-done.15 = bf16[16,6,1,256]{3,2,1,0:T(2,128)(2,1)S(1)} collective-permute-done((bf16[16,6,1,256]{3,2,1,0:T(2,128)(2,1)S(1)}, bf16[16,6,1,256]{3,2,1,0:T(2,128)(2,1)S(1)}, u32[]{:S(2)}, u32[]{:S(2)}) %collective-permute-start.15) | collective-permute-done | bytes 49184 | tf_op jit(solution)/shard_map/ppermute | solution.py:21
  160.9 11.9 %select_reduce_fusion = (f32[16]{0:T(128)S(1)}, f32[16,4,64,256]{3,2,1,0:T(8,128)}) fusion(pred[4,64,256]{2,1,0:T(8,128)(4,1)S(1)} %get-tuple-element.46, bf16[2,16,4,64,256]{4,3,2,1,0:T(8,128)(2,1)S(1)} %copy-done.2, f32[16]{0:T(128)S(1)} %neg.25, bf16[16,4,64,256]{3,2,1,0:T(8,128)(2,1)S(1)} %fusion.51, f32[16,4,64,255]{3,2,1,0:T(8,128)S(1)} %get-tuple-element.20, ...), kind=kLoop, calls=%fused_computation.64 | loop fusion | flops 59768816 | bytes 19562624 | tf_op jit(solution)/shard_map/reduce_sum | solution.py:66
  172.9 38.2 %psum.7 = f32[16]{0:T(128)S(1)} all-reduce(f32[16]{0:T(128)S(1)} %get-tuple-element.4), channel_id=1, replica_groups=mesh['gx'=8,'gy'=4] {'gx','gy'}, use_global_device_ids=true, to_apply=%region_1.2 | all-reduce | flops 16 | bytes 128 | tf_op jit(solution)/shard_map/psum | solution.py:67
  211.3 2.9 %add_convert_fusion.1 = (bf16[8,1,4,64,256]{4,3,2,1,0:T(8,128)(2,1)S(1)}, bf16[8,1,4,64,256]{4,3,2,1,0:T(8,128)(2,1)S(1)}) fusion(f32[8,2,4,64,256]{4,3,2,1,0:T(8,128)} %bitcast.25, f32[8]{0:T(128)S(1)} %get-tuple-element.3, f32[8]{0:T(128)S(1)} %get-tuple-element.2), kind=kLoop, calls=%fused_computation.99 | loop fusion | flops 4194304 | bytes 6291520 | tf_op jit(solution)/shard_map/convert.2
  214.3 1.5 pad_maximum_fusion.28
  (70 shorter events, 20.0 us)
Async XLA Ops:
  0.6 8.5 %copy-start = (bf16[16,4,64,256]{3,2,1,0:T(8,128)(2,1)S(1)}, bf16[16,4,64,256]{3,2,1,0:T(8,128)(2,1)}, u32[]{:S(2)}) copy-start(bf16[16,4,64,256]{3,2,1,0:T(8,128)(2,1)} %param.5) | copy-start | bytes 6291460
  3.1 25.7 %collective-permute-start.1 = (bf16[16,1,64,256]{3,2,1,0:T(8,128)(2,1)}, bf16[16,1,64,256]{3,2,1,0:T(8,128)(2,1)}, u32[]{:S(2)}, u32[]{:S(2)}) collective-permute-start(bf16[16,1,64,256]{3,2,1,0:T(8,128)(2,1)} %get-tuple-element.35), channel_id=1, source_target_pairs={{0,4},{4,8},{8,12},{12,16},{16,20},{20,24},{24,28},{28,0},{1,5},{5... | collective-permute-start | bytes 1572872 | tf_op jit(solution)/shard_map/ppermute | solution.py:21
  6.0 24.9 %collective-permute-start = (bf16[16,1,64,256]{3,2,1,0:T(8,128)(2,1)}, bf16[16,1,64,256]{3,2,1,0:T(8,128)(2,1)}, u32[]{:S(2)}, u32[]{:S(2)}) collective-permute-start(bf16[16,1,64,256]{3,2,1,0:T(8,128)(2,1)} %get-tuple-element.34), channel_id=1, source_target_pairs={{4,0},{8,4},{12,8},{16,12},{20,16},{24,20},{28,24},{0,28},{5,1},{9... | collective-permute-start | bytes 1572872 | tf_op jit(solution)/shard_map/ppermute | solution.py:23
  14.7 22.7 %copy-start.4 = (f32[16,4,64,255]{3,2,1,0:T(8,128)S(1)}, f32[16,4,64,255]{3,2,1,0:T(8,128)}, u32[]{:S(2)}) copy-start(f32[16,4,64,255]{3,2,1,0:T(8,128)} %get-tuple-element.37) | copy-start | bytes 12533764
  16.1 21.3 %copy-start.3 = (f32[16,4,64,255]{3,2,1,0:T(8,128)S(1)}, f32[16,4,64,255]{3,2,1,0:T(8,128)}, u32[]{:S(2)}) copy-start(f32[16,4,64,255]{3,2,1,0:T(8,128)} %get-tuple-element.36) | copy-start | bytes 12533764
  16.3 102.3 %copy-start.5 = (f32[4,64,256]{2,1,0:T(8,128)}, f32[4,64,256]{2,1,0:T(8,128)S(1)}, u32[]{:S(2)}) copy-start(f32[4,64,256]{2,1,0:T(8,128)S(1)} %get-tuple-element.45) | copy-start | bytes 786436
  16.3 16.8 %copy-start.10 = (f32[16]{0:T(128)S(1)}, f32[16]{0:T(128)}, u32[]{:S(2)}) copy-start(f32[16]{0:T(128)} %param.7) | copy-start | bytes 196
  16.3 21.1 %copy-start.1 = (bf16[2,16,4,64,256]{4,3,2,1,0:T(8,128)(2,1)S(1)}, bf16[2,16,4,64,256]{4,3,2,1,0:T(8,128)(2,1)}, u32[]{:S(2)}) copy-start(bf16[2,16,4,64,256]{4,3,2,1,0:T(8,128)(2,1)} %param.8) | copy-start | bytes 12582916
  32.2 2.3 %collective-permute-start.2 = (bf16[16,6,1,256]{3,2,1,0:T(2,128)(2,1)S(1)}, bf16[16,6,1,256]{3,2,1,0:T(2,128)(2,1)S(1)}, u32[]{:S(2)}, u32[]{:S(2)}) collective-permute-start(bf16[16,6,1,256]{3,2,1,0:T(2,128)(2,1)S(1)} %get-tuple-element.14), channel_id=1, source_target_pairs={{1,0},{2,1},{3,2},{0,3},{5,4},{6,5},{7,6},{4,7},{9,8},{10,9},{11,1... | collective-permute-start | bytes 147464 | tf_op jit(solution)/shard_map/ppermute | solution.py:23
  32.3 5.1 %collective-permute-start.3 = (bf16[16,6,1,256]{3,2,1,0:T(2,128)(2,1)S(1)}, bf16[16,6,1,256]{3,2,1,0:T(2,128)(2,1)S(1)}, u32[]{:S(2)}, u32[]{:S(2)}) collective-permute-start(bf16[16,6,1,256]{3,2,1,0:T(2,128)(2,1)S(1)} %get-tuple-element.15), channel_id=1, source_target_pairs={{0,1},{1,2},{2,3},{3,0},{4,5},{5,6},{6,7},{7,4},{8,9},{9,10},{10,1... | collective-permute-start | bytes 147464 | tf_op jit(solution)/shard_map/ppermute | solution.py:21
  47.3 25.2 %collective-permute-start.4 = (bf16[16,1,64,256]{3,2,1,0:T(8,128)(2,1)S(1)}, bf16[16,1,64,256]{3,2,1,0:T(8,128)(2,1)S(1)}, u32[]{:S(2)}, u32[]{:S(2)}) collective-permute-start(bf16[16,1,64,256]{3,2,1,0:T(8,128)(2,1)S(1)} %get-tuple-element.29), channel_id=1, source_target_pairs={{4,0},{8,4},{12,8},{16,12},{20,16},{24,20},{28,24},{0,28},{5,1},{9... | collective-permute-start | bytes 1572872 | tf_op jit(solution)/shard_map/ppermute | solution.py:23
  51.9 20.6 %collective-permute-start.5 = (bf16[16,1,64,256]{3,2,1,0:T(8,128)(2,1)S(1)}, bf16[16,1,64,256]{3,2,1,0:T(8,128)(2,1)S(1)}, u32[]{:S(2)}, u32[]{:S(2)}) collective-permute-start(bf16[16,1,64,256]{3,2,1,0:T(8,128)(2,1)S(1)} %get-tuple-element.28), channel_id=1, source_target_pairs={{0,4},{4,8},{8,12},{12,16},{16,20},{20,24},{24,28},{28,0},{1,5},{5... | collective-permute-start | bytes 1572872 | tf_op jit(solution)/shard_map/ppermute | solution.py:21
  72.7 2.3 %collective-permute-start.6 = (bf16[16,6,1,256]{3,2,1,0:T(2,128)(2,1)S(1)}, bf16[16,6,1,256]{3,2,1,0:T(2,128)(2,1)S(1)}, u32[]{:S(2)}, u32[]{:S(2)}) collective-permute-start(bf16[16,6,1,256]{3,2,1,0:T(2,128)(2,1)S(1)} %get-tuple-element.12), channel_id=1, source_target_pairs={{1,0},{2,1},{3,2},{0,3},{5,4},{6,5},{7,6},{4,7},{9,8},{10,9},{11,1... | collective-permute-start | bytes 147464 | tf_op jit(solution)/shard_map/ppermute | solution.py:23
  72.7 5.1 %collective-permute-start.7 = (bf16[16,6,1,256]{3,2,1,0:T(2,128)(2,1)S(1)}, bf16[16,6,1,256]{3,2,1,0:T(2,128)(2,1)S(1)}, u32[]{:S(2)}, u32[]{:S(2)}) collective-permute-start(bf16[16,6,1,256]{3,2,1,0:T(2,128)(2,1)S(1)} %get-tuple-element.13), channel_id=1, source_target_pairs={{0,1},{1,2},{2,3},{3,0},{4,5},{5,6},{6,7},{7,4},{8,9},{9,10},{10,1... | collective-permute-start | bytes 147464 | tf_op jit(solution)/shard_map/ppermute | solution.py:21
  87.1 25.8 %collective-permute-start.8 = (bf16[16,1,64,256]{3,2,1,0:T(8,128)(2,1)S(1)}, bf16[16,1,64,256]{3,2,1,0:T(8,128)(2,1)S(1)}, u32[]{:S(2)}, u32[]{:S(2)}) collective-permute-start(bf16[16,1,64,256]{3,2,1,0:T(8,128)(2,1)S(1)} %get-tuple-element.23), channel_id=1, source_target_pairs={{4,0},{8,4},{12,8},{16,12},{20,16},{24,20},{28,24},{0,28},{5,1},{9... | collective-permute-start | bytes 1572872 | tf_op jit(solution)/shard_map/ppermute | solution.py:23
  91.7 21.4 %collective-permute-start.9 = (bf16[16,1,64,256]{3,2,1,0:T(8,128)(2,1)S(1)}, bf16[16,1,64,256]{3,2,1,0:T(8,128)(2,1)S(1)}, u32[]{:S(2)}, u32[]{:S(2)}) collective-permute-start(bf16[16,1,64,256]{3,2,1,0:T(8,128)(2,1)S(1)} %get-tuple-element.22), channel_id=1, source_target_pairs={{0,4},{4,8},{8,12},{12,16},{16,20},{20,24},{24,28},{28,0},{1,5},{5... | collective-permute-start | bytes 1572872 | tf_op jit(solution)/shard_map/ppermute | solution.py:21
  113.2 2.3 %collective-permute-start.10 = (bf16[16,6,1,256]{3,2,1,0:T(2,128)(2,1)S(1)}, bf16[16,6,1,256]{3,2,1,0:T(2,128)(2,1)S(1)}, u32[]{:S(2)}, u32[]{:S(2)}) collective-permute-start(bf16[16,6,1,256]{3,2,1,0:T(2,128)(2,1)S(1)} %get-tuple-element.10), channel_id=1, source_target_pairs={{1,0},{2,1},{3,2},{0,3},{5,4},{6,5},{7,6},{4,7},{9,8},{10,9},{11,1... | collective-permute-start | bytes 147464 | tf_op jit(solution)/shard_map/ppermute | solution.py:23
  113.3 5.3 %collective-permute-start.11 = (bf16[16,6,1,256]{3,2,1,0:T(2,128)(2,1)S(1)}, bf16[16,6,1,256]{3,2,1,0:T(2,128)(2,1)S(1)}, u32[]{:S(2)}, u32[]{:S(2)}) collective-permute-start(bf16[16,6,1,256]{3,2,1,0:T(2,128)(2,1)S(1)} %get-tuple-element.11), channel_id=1, source_target_pairs={{0,1},{1,2},{2,3},{3,0},{4,5},{5,6},{6,7},{7,4},{8,9},{9,10},{10,1... | collective-permute-start | bytes 147464 | tf_op jit(solution)/shard_map/ppermute | solution.py:21
  128.7 26.2 %collective-permute-start.12 = (bf16[16,1,64,256]{3,2,1,0:T(8,128)(2,1)}, bf16[16,1,64,256]{3,2,1,0:T(8,128)(2,1)}, u32[]{:S(2)}, u32[]{:S(2)}) collective-permute-start(bf16[16,1,64,256]{3,2,1,0:T(8,128)(2,1)} %get-tuple-element.17), channel_id=1, source_target_pairs={{4,0},{8,4},{12,8},{16,12},{20,16},{24,20},{28,24},{0,28},{5,1},{9... | collective-permute-start | bytes 1572872 | tf_op jit(solution)/shard_map/ppermute | solution.py:23
  131.8 23.2 %collective-permute-start.13 = (bf16[16,1,64,256]{3,2,1,0:T(8,128)(2,1)}, bf16[16,1,64,256]{3,2,1,0:T(8,128)(2,1)}, u32[]{:S(2)}, u32[]{:S(2)}) collective-permute-start(bf16[16,1,64,256]{3,2,1,0:T(8,128)(2,1)} %get-tuple-element.16), channel_id=1, source_target_pairs={{0,4},{4,8},{8,12},{12,16},{16,20},{20,24},{24,28},{28,0},{1,5},{5... | collective-permute-start | bytes 1572872 | tf_op jit(solution)/shard_map/ppermute | solution.py:21
  156.0 2.7 %collective-permute-start.14 = (bf16[16,6,1,256]{3,2,1,0:T(2,128)(2,1)S(1)}, bf16[16,6,1,256]{3,2,1,0:T(2,128)(2,1)S(1)}, u32[]{:S(2)}, u32[]{:S(2)}) collective-permute-start(bf16[16,6,1,256]{3,2,1,0:T(2,128)(2,1)S(1)} %get-tuple-element.8), channel_id=1, source_target_pairs={{1,0},{2,1},{3,2},{0,3},{5,4},{6,5},{7,6},{4,7},{9,8},{10,9},{11,1... | collective-permute-start | bytes 147464 | tf_op jit(solution)/shard_map/ppermute | solution.py:23
  156.1 4.8 %copy-start.2 = (bf16[2,16,4,64,256]{4,3,2,1,0:T(8,128)(2,1)S(1)}, bf16[2,16,4,64,256]{4,3,2,1,0:T(8,128)(2,1)}, u32[]{:S(2)}) copy-start(bf16[2,16,4,64,256]{4,3,2,1,0:T(8,128)(2,1)} %param.8) | copy-start | bytes 12582916
  156.1 4.8 %collective-permute-start.15 = (bf16[16,6,1,256]{3,2,1,0:T(2,128)(2,1)S(1)}, bf16[16,6,1,256]{3,2,1,0:T(2,128)(2,1)S(1)}, u32[]{:S(2)}, u32[]{:S(2)}) collective-permute-start(bf16[16,6,1,256]{3,2,1,0:T(2,128)(2,1)S(1)} %get-tuple-element.9), channel_id=1, source_target_pairs={{0,1},{1,2},{2,3},{3,0},{4,5},{5,6},{6,7},{7,4},{8,9},{9,10},{10,1... | collective-permute-start | bytes 147464 | tf_op jit(solution)/shard_map/ppermute | solution.py:21
  160.9 50.4 %copy-start.9 = (f32[8]{0:T(128)S(1)}, f32[8]{0:T(128)}, u32[]{:S(2)}) copy-start(f32[8]{0:T(128)} %param.9) | copy-start | bytes 100
  (4 other events, 15.2 us)
where the time goes:
time: 216 us
  waiting for transfers between devices  90.7 us (42%)
  other arithmetic  47.4 us (22%)
  blocking collectives  38.2 us (18%)
  starting transfers between devices  20.5 us (9%)
  local copies, waits for them, and re-layouts  18.1 us (8%)
    ppermute x8, waiting for transfers between devices, with_halo(): lax.ppermute(head, axis, [((i + 1) % count, i) for i in range(count)])  67 us
    psum x1, blocking collectives, body(): total = lax.psum(partial_sum, ('gx', 'gy'))  38.2 us
    convert_element_type x3, other arithmetic, body(): state = jnp.where(parity == colour, flipped, current).astype(jnp.bfloat16)  28 us
    ppermute x8, waiting for transfers between devices, with_halo(): lax.ppermute(tail, axis, [(i, (i + 1) % count) for i in range(count)])  23.7 us
    ppermute x8, starting transfers between devices, with_halo(): lax.ppermute(head, axis, [((i + 1) % count, i) for i in range(count)])  15.5 us
    reduce_sum x1, other arithmetic, body(): jnp.sum(jnp.where(parity == 1, current * field, 0.0), axis=(1, 2, 3))  11.9 us
    slice x6, local copies, waits for them, and re-layouts, neighbour_field(): jnp.roll(current, -1, 3)  8.56 us
    ppermute x8, starting transfers between devices, with_halo(): lax.ppermute(tail, axis, [(i, (i + 1) % count) for i in range(count)])  4.94 us
  transfers between devices with their start and end apart: 16, of which 14 were waited for; matrix products, arithmetic and copies ran while one was open for 6% of the time, Pallas kernels for 0%

commit v1 on v0

v1 whole, which is shorter than its diff:
```python
import functools

import jax
import jax.numpy as jnp
from jax import lax
from jax.experimental import pallas as pl
from jax.experimental.pallas import tpu as pltpu
from jax.sharding import PartitionSpec as P

MESH = pl.DeviceIdType.MESH
LOG2E = 1.4426950408889634
PAD = 8
ROWS = 16

soft_width = 0.1
swap_width = 0.25
swap_gain = 64.0


def kernel(
    nx, ny, group,
    spins, bonds, metro, betas, swaps,
    swept, energy_out, mix_out,
    state, weights, xsend, xrecv, ysend, yrecv, esum, erow, eslot_y, eslot_x,
    ssem, rsem, esend, erecv,
):
    replicas, cells_x, cells_y, cells_z = spins.shape
    sweeps = metro.shape[0]
    pairs = cells_x // 2
    half = cells_y // 2
    groups = replicas // group
    chunks = cells_y // ROWS
    steps = 2 * sweeps
    gx = lax.axis_index("gx")
    gy = lax.axis_index("gy")
    up_x, down_x = lax.rem(gx + 1, nx), lax.rem(gx + nx - 1, nx)
    up_y, down_y = lax.rem(gy + 1, ny), lax.rem(gy + ny - 1, ny)

    barrier = pltpu.get_barrier_semaphore()
    for k in range(1, nx):
        pl.semaphore_signal(barrier, inc=1, device_id=(lax.rem(gx + k, nx), gy), device_id_type=MESH)
    for k in range(1, ny):
        pl.semaphore_signal(barrier, inc=1, device_id=(gx, lax.rem(gy + k, ny)), device_id_type=MESH)

    yz = lax.broadcasted_iota(jnp.int32, (ROWS, cells_z), 0) + lax.broadcasted_iota(jnp.int32, (ROWS, cells_z), 1)
    even = (yz & 1) == 0

    def low(colour):
        return even if colour == 0 else jnp.logical_not(even)

    def copies(t, g):
        out = []
        for side, target in enumerate(((up_x, gy), (down_x, gy))):
            out.append(pltpu.make_async_remote_copy(
                src_ref=xsend.at[t, g, side], dst_ref=xrecv.at[t, g, side],
                send_sem=ssem.at[t, g, side], recv_sem=rsem.at[t, g, side],
                device_id=target, device_id_type=MESH))
        for side, target in enumerate(((gx, up_y), (gx, down_y))):
            out.append(pltpu.make_async_remote_copy(
                src_ref=ysend.at[t, g, side], dst_ref=yrecv.at[t, g, side],
                send_sem=ssem.at[t, g, 2 + side], recv_sem=rsem.at[t, g, 2 + side],
                device_id=target, device_id_type=MESH))
        return out

    def pack_faces(t, g, rr, r):
        colour = t % 2
        mask = low(colour)
        other = 1 - colour
        for y0 in range(0, half, ROWS):
            for side, plane in ((0, pairs - 1), (1, 0)):
                near = state[other, r, plane, pl.ds(PAD + y0, ROWS), :]
                far = pltpu.roll(state[other, r, plane, pl.ds(PAD + half + y0, ROWS), :], 1, 1)
                face = jnp.where(mask, near, far) if side == 0 else jnp.where(mask, far, near)
                xsend[t, g, side, rr, pl.ds(y0, ROWS), :] = face.astype(jnp.bfloat16)
        for i in range(pairs):
            ysend[t, g, 0, pl.ds(rr * pairs + i, 1), :] = state[other, r, i, pl.ds(PAD + cells_y - 1, 1), :]
            ysend[t, g, 1, pl.ds(rr * pairs + i, 1), :] = state[other, r, i, pl.ds(PAD, 1), :]

    def first_group(g, carry):
        def one(rr, c):
            r = g * group + rr
            for i in range(pairs):
                for n in range(chunks):
                    rows = pl.ds(n * ROWS, ROWS)
                    a = spins[r, 2 * i, rows, :].astype(jnp.float32)
                    b = spins[r, 2 * i + 1, rows, :].astype(jnp.float32)
                    state[0, r, i, pl.ds(PAD + n * ROWS, ROWS), :] = jnp.where(even, a, b)
                    state[1, r, i, pl.ds(PAD + n * ROWS, ROWS), :] = jnp.where(even, b, a)
            pack_faces(0, g, rr, r)
            return c
        lax.fori_loop(0, group, one, 0)
        for copy in copies(0, g):
            copy.start()
        return carry

    pl.semaphore_wait(barrier, nx + ny - 2)
    lax.fori_loop(0, groups, first_group, 0)

    def weigh(n, carry):
        rows = pl.ds(pl.multiple_of(n * ROWS, ROWS), ROWS)
        for colour in (0, 1):
            mask = low(colour)
            for i in range(pairs):
                lo, hi = 2 * i, 2 * i + 1
                table = ((0, 3), (3, 0), (1, 1), (4, 4), (2, 2), (5, 5))
                for k, (p, q) in enumerate(table):
                    value = jnp.where(mask, bonds[p, lo, rows, :], bonds[q, hi, rows, :])
                    weights[colour, k, i, rows, :] = value.astype(jnp.float32)
        return carry

    lax.fori_loop(0, chunks, weigh, 0)

    for t in range(steps):
        colour, sweep, other = t % 2, t // 2, 1 - t % 2
        mask = low(colour)
        last = t == steps - 1

        def one_group(g, carry, t=t, colour=colour, sweep=sweep, other=other, mask=mask, last=last):
            for copy in copies(t, g):
                copy.wait_recv()

            def one(rr, c):
                r = g * group + rr
                gain = betas[r] * (-2.0 * LOG2E)
                for i in range(pairs):
                    row = pl.ds(rr * pairs + i, 1)
                    state[other, r, i, pl.ds(PAD - 1, 1), :] = yrecv[t, g, 0, row, :]
                    state[other, r, i, pl.ds(PAD + cells_y, 1), :] = yrecv[t, g, 1, row, :]
                total = jnp.zeros((ROWS, cells_z), jnp.float32)
                for i in range(pairs):
                    for n in range(chunks):
                        y0 = n * ROWS
                        rows = pl.ds(y0, ROWS)
                        inner = pl.ds(PAD + y0, ROWS)
                        w = [weights[colour, k, i, rows, :] for k in range(6)]

                        def halo(side):
                            face = xrecv[t, g, side, rr, pl.ds(y0 % half, ROWS), :].astype(jnp.float32)
                            return face if y0 < half else pltpu.roll(face, cells_z - 1, 1)

                        mid = state[other, r, i, inner, :]
                        below = state[other, r, i - 1, inner, :] if i > 0 else halo(0)
                        above = state[other, r, i + 1, inner, :] if i < pairs - 1 else halo(1)
                        field = w[0] * mid + w[1] * jnp.where(mask, below, above)
                        field = field + w[2] * state[other, r, i, pl.ds(PAD + y0 + 1, ROWS), :]
                        field = field + w[3] * state[other, r, i, pl.ds(PAD + y0 - 1, ROWS), :]
                        field = field + w[4] * pltpu.roll(mid, cells_z - 1, 1) + w[5] * pltpu.roll(mid, 1, 1)
                        s = state[colour, r, i, inner, :]
                        u_lo = metro[sweep, r, 2 * i, rows, :].astype(jnp.float32)
                        u_hi = metro[sweep, r, 2 * i + 1, rows, :].astype(jnp.float32)
                        u = jnp.where(mask, u_lo, u_hi)
                        accept = jnp.exp2(jnp.minimum(s * field * gain, 0.0))
                        new = s * jnp.tanh((u - accept) * (0.5 / soft_width))
                        rounded = new.astype(jnp.bfloat16)
                        s = rounded.astype(jnp.float32)
                        if last:
                            total = total + s * field
                            a = jnp.where(even, mid, s)
                            b = jnp.where(even, s, mid)
                            swept[r, 2 * i, rows, :] = a.astype(jnp.bfloat16)
                            swept[r, 2 * i + 1, rows, :] = b.astype(jnp.bfloat16)
                        else:
                            state[colour, r, i, inner, :] = s
                if last:
                    esum[lax.rem(r, 2), pl.ds(r // 2, 1), :] = jnp.sum(total, axis=0, keepdims=True)
                else:
                    pack_faces(t + 1, g, rr, r)
                return c

            lax.fori_loop(0, group, one, 0)
            if not last:
                for copy in copies(t + 1, g):
                    copy.start()
            return carry

        lax.fori_loop(0, groups, one_group, 0)

    def share(value, slots, n, mine, sem0, device):
        erow[sem0] = value
        slots[mine] = value
        sends = []
        for k in range(1, n):
            copy = pltpu.make_async_remote_copy(
                src_ref=erow.at[sem0], dst_ref=slots.at[mine],
                send_sem=esend.at[sem0, k], recv_sem=erecv.at[sem0, k],
                device_id=device(lax.rem(mine + k, n)), device_id_type=MESH)
            copy.start()
            sends.append(copy)
        for copy in sends:
            copy.wait()
        total = slots[0]
        for k in range(1, n):
            total = total + slots[k]
        return total

    mine = jnp.sum(esum[...], axis=2, keepdims=True) + jnp.zeros(erow.shape[1:], jnp.float32)
    total = share(mine, eslot_y, ny, gy, 0, lambda d: (gx, d))
    total = share(total, eslot_x, nx, gx, 1, lambda d: (d, gy))
    energies = total * (-1.0 / (cells_x * nx * cells_y * ny * cells_z))
    energy_out[...] = energies
    row = lax.broadcasted_iota(jnp.int32, erow.shape[2:], 0)
    gap = jnp.zeros(erow.shape[2:], jnp.float32)
    draw = jnp.ones(erow.shape[2:], jnp.float32)
    for k in range(replicas // 2):
        gap = jnp.where(row == k, betas[2 * k] - betas[2 * k + 1], gap)
        draw = jnp.where(row == k, swaps[k], draw)
    delta = swap_gain * gap * (energies[0] - energies[1])
    mix_out[...] = jax.nn.sigmoid((jnp.minimum(delta, 0.0) - jnp.log(draw)) / swap_width)

    def finish(g, carry):
        for t in range(steps):
            for copy in copies(t, g):
                copy.wait_send()
        return carry

    lax.fori_loop(0, groups, finish, 0)


def solution(mesh):
    nx, ny = mesh.shape["gx"], mesh.shape["gy"]

    def body(spins, couplings, betas, metro_uniform, swap_uniform):
        replicas, cells_x, cells_y, cells_z = spins.shape
        sweeps = metro_uniform.shape[0]
        pairs, steps, duos = cells_x // 2, 2 * sweeps, replicas // 2
        group = 8 // pairs
        groups = replicas // group
        f32, bf16 = jnp.float32, jnp.bfloat16
        vmem = pl.BlockSpec(memory_space=pltpu.VMEM)
        smem = pl.BlockSpec(memory_space=pltpu.SMEM)
        lanes = 128
        xface = (steps, groups, 2, group, cells_y // 2, cells_z)
        yface = (steps, groups, 2, group * pairs, cells_z)
        swept, energy, mix = pl.pallas_call(
            functools.partial(kernel, nx, ny, group),
            out_shape=(
                jax.ShapeDtypeStruct(spins.shape, bf16),
                jax.ShapeDtypeStruct((2, duos, lanes), f32),
                jax.ShapeDtypeStruct((duos, lanes), f32),
            ),
            in_specs=[vmem, vmem, vmem, smem, smem],
            out_specs=(vmem, vmem, vmem),
            scratch_shapes=[
                pltpu.VMEM((2, replicas, pairs, cells_y + 2 * PAD, cells_z), f32),
                pltpu.VMEM((2, 6, pairs, cells_y, cells_z), f32),
                pltpu.VMEM(xface, bf16),
                pltpu.VMEM(xface, bf16),
                pltpu.VMEM(yface, f32),
                pltpu.VMEM(yface, f32),
                pltpu.VMEM((2, duos, cells_z), f32),
                pltpu.VMEM((2, 2, duos, lanes), f32),
                pltpu.VMEM((ny, 2, duos, lanes), f32),
                pltpu.VMEM((nx, 2, duos, lanes), f32),
                pltpu.SemaphoreType.DMA((steps, groups, 4)),
                pltpu.SemaphoreType.DMA((steps, groups, 4)),
                pltpu.SemaphoreType.DMA((2, max(nx, ny))),
                pltpu.SemaphoreType.DMA((2, max(nx, ny))),
            ],
            compiler_params=pltpu.CompilerParams(
                collective_id=0, has_side_effects=True, vmem_limit_bytes=48 * 1024 * 1024
            ),
        )(spins, couplings, metro_uniform, betas, swap_uniform)
        paired = swept.reshape(duos, 2, cells_x, cells_y, cells_z).astype(f32)
        weight = mix[:, 0][:, None, None, None, None]
        mixed = ((1.0 - weight) * paired + weight * paired[:, ::-1]).astype(bf16)
        return mixed.reshape(spins.shape), energy[:, :, 0].T.reshape(replicas)

    in_specs = (
        P(None, "gx", "gy", None),
        P(None, "gx", "gy", None),
        P(),
        P(None, None, "gx", "gy", None),
        P(),
    )
    out_specs = (P(None, "gx", "gy", None), P())
    return jax.shard_map(body, mesh=mesh, in_specs=in_specs, out_specs=out_specs, check_vma=False)
```

time: 216 us -> 72.7 us (0.34)
  waiting for transfers between devices: 90.7 us -> 0 us
  Pallas kernels: 0 us -> 64 us
  other arithmetic: 47.4 us -> 2.58 us
  blocking collectives: 38.2 us -> 0 us
  starting transfers between devices: 20.5 us -> 0 us
  local copies, waits for them, and re-layouts: 18.1 us -> 5.18 us
    ppermute x16 -> x0, waiting for transfers between devices: 90.7 us -> none  [the longest x8 67 us: with_halo(): lax.ppermute(head, axis, [((i + 1) % count, i) for i in range(count)])]
    pallas_call x0 -> x1, Pallas kernels: none -> 64 us  [body(): pl.pallas_call(functools.partial(kernel, nx, ny, group), out_shape=(jax.S...]
    psum x1 -> x0, blocking collectives: 38.2 us -> none  [body(): total = lax.psum(partial_sum, ('gx', 'gy'))]
    convert_element_type x4 -> x2, other arithmetic: 29.3 us -> 2.58 us  [the longest x1 2.04 us: body(): mixed = ((1.0 - weight) * paired + weight * paired[:, ::-1]).astype(bf16)]
    ppermute x16 -> x0, starting transfers between devices: 20.5 us -> none  [the longest x8 15.5 us: with_halo(): lax.ppermute(head, axis, [((i + 1) % count, i) for i in range(count)])]
    slice x17 -> x2, local copies, waits for them, and re-layouts: 14.7 us -> 0.2 us  [the longest x1 0.11 us: body(): weight = mix[:, 0][:, None, None, None, None]]
    reduce_sum x1 -> x0, other arithmetic: 11.9 us -> none  [body(): jnp.sum(jnp.where(parity == 1, current * field, 0.0), axis=(1, 2, 3))]
    another operation x2 -> x0, other arithmetic: 4.43 us -> none
  transfers between devices with their start and end apart: 16 -> 0, of which waited for: 14 -> 0; matrix products, arithmetic and copies ran while one was open for 6% -> 0% of each run, Pallas kernels for 0% -> 0%
where the time goes in v1:
time: 72.7 us; the launch traced here: 72.4 us
  Pallas kernels  64 us (88%)
  local copies, waits for them, and re-layouts  5.18 us (7%)
  other arithmetic  2.58 us (4%)
    pallas_call x1, Pallas kernels, body(): pl.pallas_call(functools.partial(kernel, nx, ny, group), out_shape=(jax.S...  64 us
    unnamed x8, local copies, waits for them, and re-layouts  4.3 us
    convert_element_type x1, other arithmetic, body(): mixed = ((1.0 - weight) * paired + weight * paired[:, ::-1]).astype(bf16)  2.04 us

profile of v1, /device:TPU:0, one launch (start us, length us, event | category | flops | bytes accessed | tf_op | source)
XLA Modules:
  0.0 72.4 jit_solution(12361444637832342785)
XLA Ops:
  0.6 0.0 copy-start
  0.6 1.6 %copy-done = bf16[16,4,64,256]{3,2,1,0:T(8,128)(2,1)S(1)} copy-done((bf16[16,4,64,256]{3,2,1,0:T(8,128)(2,1)S(1)}, bf16[16,4,64,256]{3,2,1,0:T(8,128)(2,1)}, u32[]{:S(2)}) %copy-start) | copy-done | bytes 2097176
  2.2 0.0 copy-start.1
  2.2 1.4 %copy-done.1 = s32[6,4,64,256]{3,2,1,0:T(8,128)S(1)} copy-done((s32[6,4,64,256]{3,2,1,0:T(8,128)S(1)}, s32[6,4,64,256]{3,2,1,0:T(8,128)}, u32[]{:S(2)}) %copy-start.1) | copy-done | bytes 1572888
  3.6 0.0 copy-start.2
  3.6 0.7 copy-done.2
  4.3 0.0 copy-start.3
  4.3 0.7 copy-done.3
  4.9 64.0 %shard_map.68 = (bf16[16,4,64,256]{3,2,1,0:T(8,128)(2,1)S(1)}, f32[2,8,128]{2,1,0:T(8,128)S(1)}, f32[8,128]{1,0:T(8,128)S(1)}) custom-call(bf16[16,4,64,256]{3,2,1,0:T(8,128)(2,1)S(1)} %copy-done, s32[6,4,64,256]{3,2,1,0:T(8,128)S(1)} %copy-done.1, bf16[2,16,4,64,256]{4,3,2,1,0:T(8,128)(2,1)} %metro.1, f32[16]{0:T(128)S(1)} %copy-done.2, f32[8]{0:T(128)S(1)} %copy-done.3), custom_call_target="tpu_custom_call" | custom-call | tf_op jit(solution)/shard_map/pallas_call | solution.py:234
  69.0 0.1 slice_reduce_fusion.1
  69.1 0.1 slice_reduce_fusion
  69.2 0.1 copy.8
  69.3 0.6 reshape.22
  69.9 0.5 convert.1
  70.4 2.0 %add_convert_fusion = bf16[8,2,4,64,256]{4,3,2,1,0:T(8,128)(2,1)} fusion(f32[8,2,4,64,256]{4,3,2,1,0:T(8,128)S(1)} %convert.1, f32[8]{0:T(128)S(1)} %slice_reduce_fusion.1, f32[8]{0:T(128)S(1)} %broadcast_subtract_fusion), kind=kLoop, calls=%fused_computation | loop fusion | flops 4194304 | bytes 6291520 | tf_op jit(solution)/shard_map/convert_element_type | solution.py:265
  (1 shorter events, 0.0 us)
Async XLA Ops:
  0.6 1.6 %copy-start = (bf16[16,4,64,256]{3,2,1,0:T(8,128)(2,1)S(1)}, bf16[16,4,64,256]{3,2,1,0:T(8,128)(2,1)}, u32[]{:S(2)}) copy-start(bf16[16,4,64,256]{3,2,1,0:T(8,128)(2,1)} %spins.1) | copy-start | bytes 6291460
  2.2 1.4 %copy-start.1 = (s32[6,4,64,256]{3,2,1,0:T(8,128)S(1)}, s32[6,4,64,256]{3,2,1,0:T(8,128)}, u32[]{:S(2)}) copy-start(s32[6,4,64,256]{3,2,1,0:T(8,128)} %bonds.1) | copy-start | bytes 4718596
  3.6 0.7 copy-start.2
  4.3 0.7 copy-start.3

commit v2 on v1

--- a/solution.py
+++ b/solution.py
@@ -19,8 +19,9 @@
 
 def kernel(
     nx, ny, group,
-    spins, bonds, metro, betas, swaps,
-    swept, energy_out, mix_out,
+    spins_hbm, bonds_hbm, metro_hbm, betas, swaps,
+    swept_hbm, info_out,
+    spins, bonds, metro, swept, spins_sem, bonds_sem, metro_sem, swept_sem,
     state, weights, xsend, xrecv, ysend, yrecv, esum, erow, eslot_y, eslot_x,
     ssem, rsem, esend, erecv,
 ):
@@ -36,11 +37,33 @@
     up_x, down_x = lax.rem(gx + 1, nx), lax.rem(gx + nx - 1, nx)
     up_y, down_y = lax.rem(gy + 1, ny), lax.rem(gy + ny - 1, ny)
 
+    def part(g):
+        return pl.ds(g * group, group)
+
+    def spins_in(g):
+        return pltpu.make_async_copy(spins_hbm.at[part(g)], spins.at[part(g)], spins_sem.at[g])
+
+    def metro_in(sweep, g):
+        return pltpu.make_async_copy(
+            metro_hbm.at[sweep, part(g)], metro.at[sweep, part(g)], metro_sem.at[sweep, g])
+
+    def swept_to(g):
+        return pltpu.make_async_copy(swept.at[part(g)], swept_hbm.at[part(g)], swept_sem.at[g])
+
+    bonds_in = pltpu.make_async_copy(bonds_hbm, bonds, bonds_sem)
+    for g in range(groups):
+        spins_in(g).start()
+
     barrier = pltpu.get_barrier_semaphore()
     for k in range(1, nx):
         pl.semaphore_signal(barrier, inc=1, device_id=(lax.rem(gx + k, nx), gy), device_id_type=MESH)
     for k in range(1, ny):
         pl.semaphore_signal(barrier, inc=1, device_id=(gx, lax.rem(gy + k, ny)), device_id_type=MESH)
+
+    bonds_in.start()
+    for sweep in range(sweeps):
+        for g in range(groups):
+            metro_in(sweep, g).start()
 
     yz = lax.broadcasted_iota(jnp.int32, (ROWS, cells_z), 0) + lax.broadcasted_iota(jnp.int32, (ROWS, cells_z), 1)
     even = (yz & 1) == 0
@@ -76,7 +99,9 @@
             ysend[t, g, 0, pl.ds(rr * pairs + i, 1), :] = state[other, r, i, pl.ds(PAD + cells_y - 1, 1), :]
             ysend[t, g, 1, pl.ds(rr * pairs + i, 1), :] = state[other, r, i, pl.ds(PAD, 1), :]
 
-    def first_group(g, carry):
+    def prepare(g):
+        spins_in(g).wait()
+
         def one(rr, c):
             r = g * group + rr
             for i in range(pairs):
@@ -89,12 +114,19 @@
             pack_faces(0, g, rr, r)
             return c
         lax.fori_loop(0, group, one, 0)
+
+    def first_group(g, carry):
+        prepare(g)
         for copy in copies(0, g):
             copy.start()
         return carry
 
+    prepare(0)
     pl.semaphore_wait(barrier, nx + ny - 2)
-    lax.fori_loop(0, groups, first_group, 0)
+    for copy in copies(0, 0):
+        copy.start()
+    lax.fori_loop(1, groups, first_group, 0)
+    bonds_in.wait()
 
     def weigh(n, carry):
         rows = pl.ds(pl.multiple_of(n * ROWS, ROWS), ROWS)
@@ -116,6 +148,8 @@
         last = t == steps - 1
 
         def one_group(g, carry, t=t, colour=colour, sweep=sweep, other=other, mask=mask, last=last):
+            if colour == 0:
+                metro_in(sweep, g).wait()
             for copy in copies(t, g):
                 copy.wait_recv()
 
@@ -168,9 +202,13 @@
                 return c
 
             lax.fori_loop(0, group, one, 0)
-            if not last:
+            if last:
+                swept_to(g).start()
+            else:
                 for copy in copies(t + 1, g):
                     copy.start()
+            for copy in copies(t, g):
+                copy.wait_send()
             return carry
 
         lax.fori_loop(0, groups, one_group, 0)
@@ -197,7 +235,6 @@
     total = share(mine, eslot_y, ny, gy, 0, lambda d: (gx, d))
     total = share(total, eslot_x, nx, gx, 1, lambda d: (d, gy))
     energies = total * (-1.0 / (cells_x * nx * cells_y * ny * cells_z))
-    energy_out[...] = energies
     row = lax.broadcasted_iota(jnp.int32, erow.shape[2:], 0)
     gap = jnp.zeros(erow.shape[2:], jnp.float32)
     draw = jnp.ones(erow.shape[2:], jnp.float32)
@@ -205,15 +242,29 @@
         gap = jnp.where(row == k, betas[2 * k] - betas[2 * k + 1], gap)
         draw = jnp.where(row == k, swaps[k], draw)
     delta = swap_gain * gap * (energies[0] - energies[1])
-    mix_out[...] = jax.nn.sigmoid((jnp.minimum(delta, 0.0) - jnp.log(draw)) / swap_width)
-
-    def finish(g, carry):
-        for t in range(steps):
-            for copy in copies(t, g):
-                copy.wait_send()
-        return carry
-
-    lax.fori_loop(0, groups, finish, 0)
+    mix = jax.nn.sigmoid((jnp.minimum(delta, 0.0) - jnp.log(draw)) / swap_width)
+    lane = lax.broadcasted_iota(jnp.int32, erow.shape[2:], 1)
+    spread = jnp.where(lane == 2 * row, energies[0], 0.0) + jnp.where(lane == 2 * row + 1, energies[1], 0.0)
+    info_out[0:1, :] = jnp.sum(spread, axis=0, keepdims=True)
+    info_out[1:2, :] = jnp.sum(jnp.where(lane == row, mix, 0.0), axis=0, keepdims=True)
+    for g in range(groups):
+        swept_to(g).wait()
+
+
+def exchange(per, info, swept, out, energy_out):
+    step = pl.program_id(0)
+
+    @pl.when(step == 0)
+    def _():
+        for r in range(energy_out.shape[0]):
+            energy_out[r] = info[0, r]
+
+    for k in range(per):
+        weight = info[1, step * per + k]
+        upper = swept[2 * k].astype(jnp.float32)
+        lower = swept[2 * k + 1].astype(jnp.float32)
+        out[2 * k] = ((1.0 - weight) * upper + weight * lower).astype(jnp.bfloat16)
+        out[2 * k + 1] = ((1.0 - weight) * lower + weight * upper).astype(jnp.bfloat16)
 
 
 def solution(mesh):
@@ -227,20 +278,28 @@
         groups = replicas // group
         f32, bf16 = jnp.float32, jnp.bfloat16
         vmem = pl.BlockSpec(memory_space=pltpu.VMEM)
+        hbm = pl.BlockSpec(memory_space=pl.ANY)
         smem = pl.BlockSpec(memory_space=pltpu.SMEM)
         lanes = 128
         xface = (steps, groups, 2, group, cells_y // 2, cells_z)
         yface = (steps, groups, 2, group * pairs, cells_z)
-        swept, energy, mix = pl.pallas_call(
+        swept, info = pl.pallas_call(
             functools.partial(kernel, nx, ny, group),
             out_shape=(
                 jax.ShapeDtypeStruct(spins.shape, bf16),
-                jax.ShapeDtypeStruct((2, duos, lanes), f32),
-                jax.ShapeDtypeStruct((duos, lanes), f32),
+                jax.ShapeDtypeStruct((2, lanes), f32),
             ),
-            in_specs=[vmem, vmem, vmem, smem, smem],
-            out_specs=(vmem, vmem, vmem),
+            in_specs=[hbm, hbm, hbm, smem, smem],
+            out_specs=(hbm, vmem),
             scratch_shapes=[
+                pltpu.VMEM(spins.shape, bf16),
+                pltpu.VMEM(couplings.shape, jnp.int32),
+                pltpu.VMEM(metro_uniform.shape, bf16),
+                pltpu.VMEM(spins.shape, bf16),
+                pltpu.SemaphoreType.DMA((groups,)),
+                pltpu.SemaphoreType.DMA,
+                pltpu.SemaphoreType.DMA((sweeps, groups)),
+                pltpu.SemaphoreType.DMA((groups,)),
                 pltpu.VMEM((2, replicas, pairs, cells_y + 2 * PAD, cells_z), f32),
                 pltpu.VMEM((2, 6, pairs, cells_y, cells_z), f32),
                 pltpu.VMEM(xface, bf16),
@@ -257,13 +316,21 @@
                 pltpu.SemaphoreType.DMA((2, max(nx, ny))),
             ],
             compiler_params=pltpu.CompilerParams(
-                collective_id=0, has_side_effects=True, vmem_limit_bytes=48 * 1024 * 1024
+                collective_id=0, has_side_effects=True, vmem_limit_bytes=60 * 1024 * 1024
             ),
         )(spins, couplings, metro_uniform, betas, swap_uniform)
-        paired = swept.reshape(duos, 2, cells_x, cells_y, cells_z).astype(f32)
-        weight = mix[:, 0][:, None, None, None, None]
-        mixed = ((1.0 - weight) * paired + weight * paired[:, ::-1]).astype(bf16)
-        return mixed.reshape(spins.shape), energy[:, :, 0].T.reshape(replicas)
+        per = 2
+        block = pl.BlockSpec((2 * per,) + spins.shape[1:], lambda k: (k, 0, 0, 0))
+        return pl.pallas_call(
+            functools.partial(exchange, per),
+            grid=(duos // per,),
+            out_shape=(
+                jax.ShapeDtypeStruct(spins.shape, bf16),
+                jax.ShapeDtypeStruct((replicas,), f32),
+            ),
+            in_specs=[smem, block],
+            out_specs=(block, smem),
+        )(info, swept)
 
     in_specs = (
         P(None, "gx", "gy", None),

time: 72.7 us -> 68.9 us (0.948)
  local copies, waits for them, and re-layouts: 5.18 us -> 0 us
  Pallas kernels: 64 us -> 68 us
  other arithmetic: 2.58 us -> 0 us
    unnamed x8 -> x0, local copies, waits for them, and re-layouts: 4.3 us -> none
    pallas_call x0 -> x1, Pallas kernels: none -> 4.12 us  [body(): pl.pallas_call(functools.partial(exchange, per), grid=(duos // per,), out...]
    convert_element_type x2 -> x0, other arithmetic: 2.58 us -> none  [the longest x1 2.04 us: body(): mixed = ((1.0 - weight) * paired + weight * paired[:, ::-1]).astype(bf16)]
where the time goes in v2:
time: 68.9 us; the launch traced here: 68.7 us
  Pallas kernels  68 us (99%)
    pallas_call x1, Pallas kernels, body(): pl.pallas_call(functools.partial(kernel, nx, ny, group), out_shape=(jax.S...  63.9 us
    pallas_call x1, Pallas kernels, body(): pl.pallas_call(functools.partial(exchange, per), grid=(duos // per,), out...  4.12 us

profile of v2, /device:TPU:0, one launch (start us, length us, event | category | flops | bytes accessed | tf_op | source)
XLA Modules:
  0.0 68.7 jit_solution(17127173809231286104)
XLA Ops:
  0.6 63.9 %shard_map.68 = (bf16[16,4,64,256]{3,2,1,0:T(8,128)(2,1)}, f32[2,128]{1,0:T(2,128)}) custom-call(bf16[16,4,64,256]{3,2,1,0:T(8,128)(2,1)} %spins_hbm.1, s32[6,4,64,256]{3,2,1,0:T(8,128)} %bonds_hbm.1, bf16[2,16,4,64,256]{4,3,2,1,0:T(8,128)(2,1)} %metro_hbm.1, f32[16]{0:T(128)} %betas.1, f32[8]{0:T(128)} %swaps.1), custom_call_target="tpu_custom_call" | custom-call | tf_op jit(solution)/shard_map/pallas_call | solution.py:286
  64.5 4.1 %shard_map.69 = (bf16[16,4,64,256]{3,2,1,0:T(8,128)(2,1)}, f32[16]{0:T(128)}) custom-call(f32[2,128]{1,0:T(2,128)} %get-tuple-element.4.info, bf16[16,4,64,256]{3,2,1,0:T(8,128)(2,1)} %get-tuple-element.5.swept), custom_call_target="tpu_custom_call" | custom-call | tf_op jit(solution)/shard_map/pallas_call | solution.py:324

commit v3 on v2

--- a/solution.py
+++ b/solution.py
@@ -274,7 +274,7 @@
         replicas, cells_x, cells_y, cells_z = spins.shape
         sweeps = metro_uniform.shape[0]
         pairs, steps, duos = cells_x // 2, 2 * sweeps, replicas // 2
-        group = 8 // pairs
+        group = 4 // pairs
         groups = replicas // group
         f32, bf16 = jnp.float32, jnp.bfloat16
         vmem = pl.BlockSpec(memory_space=pltpu.VMEM)
@@ -319,7 +319,7 @@
                 collective_id=0, has_side_effects=True, vmem_limit_bytes=60 * 1024 * 1024
             ),
         )(spins, couplings, metro_uniform, betas, swap_uniform)
-        per = 2
+        per = 4
         block = pl.BlockSpec((2 * per,) + spins.shape[1:], lambda k: (k, 0, 0, 0))
         return pl.pallas_call(
             functools.partial(exchange, per),

time: 68.9 us -> 67.6 us (0.981)
  Pallas kernels: 68 us -> 66.8 us
    pallas_call x1, Pallas kernels: 4.12 us -> 3.01 us  [body(): pl.pallas_call(functools.partial(exchange, per), grid=(duos // per,), out...]
where the time goes in v3:
time: 67.6 us; the launch traced here: 67.4 us
  Pallas kernels  66.8 us (99%)
    pallas_call x1, Pallas kernels, body(): pl.pallas_call(functools.partial(kernel, nx, ny, group), out_shape=(jax.S...  63.8 us
    pallas_call x1, Pallas kernels, body(): pl.pallas_call(functools.partial(exchange, per), grid=(duos // per,), out...  3.01 us

profile of v3, /device:TPU:0, one launch (start us, length us, event | category | flops | bytes accessed | tf_op | source)
XLA Modules:
  0.0 67.4 jit_solution(2498916005765733717)
XLA Ops:
  0.6 63.8 %shard_map.68 = (bf16[16,4,64,256]{3,2,1,0:T(8,128)(2,1)}, f32[2,128]{1,0:T(2,128)}) custom-call(bf16[16,4,64,256]{3,2,1,0:T(8,128)(2,1)} %spins_hbm.1, s32[6,4,64,256]{3,2,1,0:T(8,128)} %bonds_hbm.1, bf16[2,16,4,64,256]{4,3,2,1,0:T(8,128)(2,1)} %metro_hbm.1, f32[16]{0:T(128)} %betas.1, f32[8]{0:T(128)} %swaps.1), custom_call_target="tpu_custom_call" | custom-call | tf_op jit(solution)/shard_map/pallas_call | solution.py:286
  64.4 3.0 %shard_map.69 = (bf16[16,4,64,256]{3,2,1,0:T(8,128)(2,1)}, f32[16]{0:T(128)}) custom-call(f32[2,128]{1,0:T(2,128)} %get-tuple-element.4.info, bf16[16,4,64,256]{3,2,1,0:T(8,128)(2,1)} %get-tuple-element.5.swept), custom_call_target="tpu_custom_call" | custom-call | tf_op jit(solution)/shard_map/pallas_call | solution.py:324

commit v4 on v3

--- a/solution.py
+++ b/solution.py
@@ -60,11 +60,6 @@
     for k in range(1, ny):
         pl.semaphore_signal(barrier, inc=1, device_id=(gx, lax.rem(gy + k, ny)), device_id_type=MESH)
 
-    bonds_in.start()
-    for sweep in range(sweeps):
-        for g in range(groups):
-            metro_in(sweep, g).start()
-
     yz = lax.broadcasted_iota(jnp.int32, (ROWS, cells_z), 0) + lax.broadcasted_iota(jnp.int32, (ROWS, cells_z), 1)
     even = (yz & 1) == 0
 
@@ -125,6 +120,10 @@
     pl.semaphore_wait(barrier, nx + ny - 2)
     for copy in copies(0, 0):
         copy.start()
+    bonds_in.start()
+    for sweep in range(sweeps):
+        for g in range(groups):
+            metro_in(sweep, g).start()
     lax.fori_loop(1, groups, first_group, 0)
     bonds_in.wait()
 

time: 67.6 us -> 67.6 us (level)
  no operation moved by 1% of the time
where the time goes in v4:
time: 67.6 us; the launch traced here: 67.4 us
  Pallas kernels  66.8 us (99%)
    pallas_call x1, Pallas kernels, body(): pl.pallas_call(functools.partial(kernel, nx, ny, group), out_shape=(jax.S...  63.8 us
    pallas_call x1, Pallas kernels, body(): pl.pallas_call(functools.partial(exchange, per), grid=(duos // per,), out...  3.01 us

profile of v4, /device:TPU:0, one launch (start us, length us, event | category | flops | bytes accessed | tf_op | source)
XLA Modules:
  0.0 67.4 jit_solution(246872662722896113)
XLA Ops:
  0.6 63.8 %shard_map.68 = (bf16[16,4,64,256]{3,2,1,0:T(8,128)(2,1)}, f32[2,128]{1,0:T(2,128)}) custom-call(bf16[16,4,64,256]{3,2,1,0:T(8,128)(2,1)} %spins_hbm.1, s32[6,4,64,256]{3,2,1,0:T(8,128)} %bonds_hbm.1, bf16[2,16,4,64,256]{4,3,2,1,0:T(8,128)(2,1)} %metro_hbm.1, f32[16]{0:T(128)} %betas.1, f32[8]{0:T(128)} %swaps.1), custom_call_target="tpu_custom_call" | custom-call | tf_op jit(solution)/shard_map/pallas_call | solution.py:285
  64.4 3.0 %shard_map.69 = (bf16[16,4,64,256]{3,2,1,0:T(8,128)(2,1)}, f32[16]{0:T(128)}) custom-call(f32[2,128]{1,0:T(2,128)} %get-tuple-element.4.info, bf16[16,4,64,256]{3,2,1,0:T(8,128)(2,1)} %get-tuple-element.5.swept), custom_call_target="tpu_custom_call" | custom-call | tf_op jit(solution)/shard_map/pallas_call | solution.py:323

commit v5 on v3

--- a/solution.py
+++ b/solution.py
@@ -73,15 +73,15 @@
 
     def copies(t, g):
         out = []
+        for side, target in enumerate(((gx, up_y), (gx, down_y))):
+            out.append(pltpu.make_async_remote_copy(
+                src_ref=ysend.at[t, g, side], dst_ref=yrecv.at[t, g, side],
+                send_sem=ssem.at[t, g, 2 + side], recv_sem=rsem.at[t, g, 2 + side],
+                device_id=target, device_id_type=MESH))
         for side, target in enumerate(((up_x, gy), (down_x, gy))):
             out.append(pltpu.make_async_remote_copy(
                 src_ref=xsend.at[t, g, side], dst_ref=xrecv.at[t, g, side],
                 send_sem=ssem.at[t, g, side], recv_sem=rsem.at[t, g, side],
-                device_id=target, device_id_type=MESH))
-        for side, target in enumerate(((gx, up_y), (gx, down_y))):
-            out.append(pltpu.make_async_remote_copy(
-                src_ref=ysend.at[t, g, side], dst_ref=yrecv.at[t, g, side],
-                send_sem=ssem.at[t, g, 2 + side], recv_sem=rsem.at[t, g, 2 + side],
                 device_id=target, device_id_type=MESH))
         return out
 

time: 67.6 us -> 67.6 us (level)
  no operation moved by 1% of the time
where the time goes in v5:
time: 67.6 us; the launch traced here: 67.4 us
  Pallas kernels  66.8 us (99%)
    pallas_call x1, Pallas kernels, body(): pl.pallas_call(functools.partial(kernel, nx, ny, group), out_shape=(jax.S...  63.8 us
    pallas_call x1, Pallas kernels, body(): pl.pallas_call(functools.partial(exchange, per), grid=(duos // per,), out...  3.01 us

profile of v5, /device:TPU:0, one launch (start us, length us, event | category | flops | bytes accessed | tf_op | source)
XLA Modules:
  0.0 67.4 jit_solution(7329763022310445501)
XLA Ops:
  0.6 63.8 %shard_map.68 = (bf16[16,4,64,256]{3,2,1,0:T(8,128)(2,1)}, f32[2,128]{1,0:T(2,128)}) custom-call(bf16[16,4,64,256]{3,2,1,0:T(8,128)(2,1)} %spins_hbm.1, s32[6,4,64,256]{3,2,1,0:T(8,128)} %bonds_hbm.1, bf16[2,16,4,64,256]{4,3,2,1,0:T(8,128)(2,1)} %metro_hbm.1, f32[16]{0:T(128)} %betas.1, f32[8]{0:T(128)} %swaps.1), custom_call_target="tpu_custom_call" | custom-call | tf_op jit(solution)/shard_map/pallas_call | solution.py:286
  64.4 3.0 %shard_map.69 = (bf16[16,4,64,256]{3,2,1,0:T(8,128)(2,1)}, f32[16]{0:T(128)}) custom-call(f32[2,128]{1,0:T(2,128)} %get-tuple-element.4.info, bf16[16,4,64,256]{3,2,1,0:T(8,128)(2,1)} %get-tuple-element.5.swept), custom_call_target="tpu_custom_call" | custom-call | tf_op jit(solution)/shard_map/pallas_call | solution.py:324
